TPU v7x, 32 devices: a whole 2x2x4 slice. The times are simulated.
32 devices in a mesh: dp: 8 (over y, x, core), gene: 4 (over z).
Axes of the slice: x: 2, y: 2, z: 4, core: 2. Of those that a mesh axis runs over, the one named last changes fastest.
Arguments:
- gene_counts: bfloat16 [4096, 13500], P('dp', 'gene'), may hold values from -6 to 6
- coords: float32 [2, 4096], P(None, ('dp', 'gene')), may hold values from 0 to 100
- lengths: int32 [8, 2], P('dp'), may hold values from 0 to 512, as said below
- enc_weight: bfloat16 [13500, 1024], P('gene'), may hold values from -0.0546875 to 0.0546875
- dec_weight: bfloat16 [1024, 13500], P(None, 'gene'), may hold values from -0.1875 to 0.1875
- attn_weight: bfloat16 [4096, 1024], P(('dp', 'gene'))
- up_weight: bfloat16 [4096, 1024], P(('dp', 'gene')), may hold values from -0.1875 to 0.1875
- down_weight: bfloat16 [4096, 1024], P(('dp', 'gene')), may hold values from -0.09375 to 0.09375
- ln_gain: bfloat16 [2048], P(('dp', 'gene')), may hold values from 0.5 to 1.5
- ln_bias: bfloat16 [2048], P(('dp', 'gene')), may hold values from -1.5 to 1.5
- logit_grad: bfloat16 [4096, 13500], P('dp', 'gene'), may hold values from -6 to 6
Outputs:
- logits: bfloat16 [4096, 13500], P('dp', 'gene')
- gene_grad: bfloat16 [4096, 13500], P('dp', 'gene')
- enc_grad: float32 [13500, 1024], P('gene', 'dp')
- dec_grad: float32 [1024, 13500], P('dp', 'gene')
- attn_grad: float32 [4096, 1024], P(('dp', 'gene'))
- up_grad: float32 [4096, 1024], P(('dp', 'gene'))
- down_grad: float32 [4096, 1024], P(('dp', 'gene'))
- gain_grad: float32 [2048], P(('dp', 'gene'))
- bias_grad: float32 [1024], P(('dp', 'gene'))
- mid_bias_grad: float32 [1024], P(('dp', 'gene'))
Inputs may be any that keep to these rules, and one draw needn't show every extreme that they name: Per group the two lengths and the padding fill 4 * 128 slots; one of the two slides covers the group's slots from below 128 to beyond 3 * 128.
All inputs are finite; a program needn't handle non-finite values.
Results may differ from a plain program's by a relative error of at most 0.03.
Values may be sent and summed in bfloat16 or wider, within the bound.
A program may use at most 192 MiB of HBM per device.

v0:
```python
import math

import jax
import jax.numpy as jnp
from jax import lax
from jax.sharding import PartitionSpec as P

HEADS = 16
HEAD_DIM = 64


epsilon = 1e-05


def norm_rows(values, gain, offset):
    center = values - jnp.mean(values, axis=-1, keepdims=True)
    spread = jnp.mean(center * center, axis=-1, keepdims=True)
    return center * lax.rsqrt(spread + epsilon) * gain + offset


def gelu_tanh(values):
    return jax.nn.gelu(values, approximate=True)


def positions(coords, model_width):
    indices = jnp.arange(model_width // 4).astype(coords.dtype)
    freqs = jnp.exp(indices * (-4.0 * math.log(10000.0) / model_width))
    along_x = coords[0][:, None] * freqs[None, :]
    along_y = coords[1][:, None] * freqs[None, :]
    return jnp.concatenate(
        [jnp.sin(along_x), jnp.cos(along_x), jnp.sin(along_y), jnp.cos(along_y)], axis=1
    )


def slide_ids(slide_lengths, length_all):
    places = jnp.arange(length_all, dtype=jnp.int32)
    return (places >= slide_lengths[0]).astype(jnp.int32) + (
        places >= slide_lengths[0] + slide_lengths[1]
    ).astype(jnp.int32)


def product(left, right):
    return jnp.dot(left, right, preferred_element_type=jnp.float32)


def contract_rows(left, right):
    return lax.dot_general(
        left, right, (((0,), (0,)), ((), ())), preferred_element_type=jnp.float32
    )


def contract_cols(left, right):
    return lax.dot_general(
        left, right, (((1,), (1,)), ((), ())), preferred_element_type=jnp.float32
    )


def body(
    gene_counts,
    coords,
    lengths,
    enc_weight,
    dec_weight,
    attn_weight,
    up_weight,
    down_weight,
    ln_gain,
    ln_bias,
    logit_grad,
):
    model_width = enc_weight.shape[1]
    group_rows = gene_counts.shape[0]
    own_rows = coords.shape[1]
    gene_index = lax.axis_index("gene")
    score_scale = 1.0 / math.sqrt(HEAD_DIM)
    slide_all = slide_ids(lengths[0], group_rows)
    slide_own = lax.dynamic_slice_in_dim(slide_all, gene_index * own_rows, own_rows)
    live_rows = (slide_all < 2).astype(jnp.bfloat16)[:, None]
    attn_full, up_full, down_full, gain_full, bias_full = (
        lax.all_gather(attn_weight, ("dp", "gene"), axis=0, tiled=True),
        lax.all_gather(up_weight, ("dp", "gene"), axis=0, tiled=True),
        lax.all_gather(down_weight, ("dp", "gene"), axis=0, tiled=True),
        lax.all_gather(ln_gain, ("dp", "gene"), axis=0, tiled=True),
        lax.all_gather(ln_bias, ("dp", "gene"), axis=0, tiled=True),
    )
    norm_gains = gain_full.astype(jnp.float32)
    offsets = bias_full.astype(jnp.float32)
    proj_weight = attn_full[: 3 * model_width]
    out_weight = attn_full[3 * model_width :]
    embedded = lax.psum_scatter(
        product(gene_counts, enc_weight).astype(jnp.bfloat16),
        "gene",
        scatter_dimension=0,
        tiled=True,
    ).astype(jnp.float32)
    stream_in = embedded + positions(coords, model_width)
    first_normed, first_pull = jax.vjp(
        norm_rows, stream_in, norm_gains[:model_width], offsets[:model_width]
    )
    first_low = first_normed.astype(jnp.bfloat16)
    projected = contract_cols(first_low, proj_weight).astype(jnp.bfloat16)
    queries = projected[:, :model_width].reshape(own_rows, HEADS, HEAD_DIM)
    keyval_all = lax.all_gather(projected[:, model_width:], "gene", axis=0, tiled=True)
    keys_all = keyval_all[:, :model_width].reshape(group_rows, HEADS, HEAD_DIM)
    values_all = keyval_all[:, model_width:].reshape(group_rows, HEADS, HEAD_DIM)
    same_slide = (slide_own[:, None] == slide_all[None, :])[None]
    scores = (
        jnp.einsum("qhd,khd->hqk", queries, keys_all, preferred_element_type=jnp.float32)
        * score_scale
    )
    scores = jnp.where(same_slide, scores, -1e30)
    row_max = jnp.max(scores, axis=-1, keepdims=True)
    raised = jnp.exp(scores - row_max)
    soft = raised / jnp.sum(raised, axis=-1, keepdims=True)
    soft_low = soft.astype(jnp.bfloat16)
    attended = jnp.einsum("hqk,khd->qhd", soft_low, values_all, preferred_element_type=jnp.float32)
    attended = attended.reshape(own_rows, model_width).astype(jnp.bfloat16)
    stream_mid = stream_in + product(attended, out_weight)
    second_normed, second_pull = jax.vjp(
        norm_rows, stream_mid, norm_gains[model_width:], offsets[model_width:]
    )
    second_low = second_normed.astype(jnp.bfloat16)
    hidden_pre = contract_cols(second_low, up_full)
    active, gelu_pull = jax.vjp(gelu_tanh, hidden_pre)
    active_low = active.astype(jnp.bfloat16)
    stream_out = stream_mid + product(active_low, down_full)
    cells_low = stream_out.astype(jnp.bfloat16)
    cells_all = lax.all_gather(cells_low, "gene", axis=0, tiled=True)
    logits_full = product(cells_all, dec_weight)
    logits = (logits_full * live_rows.astype(jnp.float32)).astype(jnp.bfloat16)
    masked_grad = logit_grad * live_rows
    grad_out = lax.psum_scatter(
        contract_cols(masked_grad, dec_weight).astype(jnp.bfloat16),
        "gene",
        scatter_dimension=0,
        tiled=True,
    ).astype(jnp.float32)
    dec_part = contract_rows(cells_all, masked_grad)
    grad_branch = grad_out.astype(jnp.bfloat16)
    down_part = contract_rows(active_low, grad_branch)
    grad_active = contract_cols(grad_branch, down_full)
    grad_hidden = gelu_pull(grad_active)[0].astype(jnp.bfloat16)
    up_part = contract_rows(grad_hidden, second_low)
    grad_second = product(grad_hidden, up_full)
    grad_mid_norm, gain_second, bias_second = second_pull(grad_second)
    grad_mid = grad_out + grad_mid_norm
    grad_attn = grad_mid.astype(jnp.bfloat16)
    out_part = contract_rows(attended, grad_attn)
    grad_attended = (
        contract_cols(grad_attn, out_weight).astype(jnp.bfloat16).reshape(own_rows, HEADS, HEAD_DIM)
    )
    grad_soft = jnp.einsum(
        "qhd,khd->hqk", grad_attended, values_all, preferred_element_type=jnp.float32
    )
    grad_scores = soft * (grad_soft - jnp.sum(grad_soft * soft, axis=-1, keepdims=True))
    grad_scores = grad_scores.astype(jnp.bfloat16)
    grad_query = (
        jnp.einsum("hqk,khd->qhd", grad_scores, keys_all, preferred_element_type=jnp.float32)
        * score_scale
    )
    grad_query = grad_query.reshape(own_rows, model_width).astype(jnp.bfloat16)
    grad_keys = (
        jnp.einsum("hqk,qhd->khd", grad_scores, queries, preferred_element_type=jnp.float32)
        * score_scale
    )
    grad_values = jnp.einsum(
        "hqk,qhd->khd", soft_low, grad_attended, preferred_element_type=jnp.float32
    )
    keyval_part = jnp.concatenate(
        [grad_keys.reshape(group_rows, model_width), grad_values.reshape(group_rows, model_width)],
        axis=1,
    )
    grad_keyval = lax.psum_scatter(
        keyval_part.astype(jnp.bfloat16), "gene", scatter_dimension=0, tiled=True
    )
    grad_proj = jnp.concatenate([grad_query, grad_keyval], axis=1)
    proj_part = contract_rows(grad_proj, first_low)
    grad_first = product(grad_proj, proj_weight)
    grad_in_norm, gain_first, bias_first = first_pull(grad_first)
    grad_in = (grad_mid + grad_in_norm).astype(jnp.bfloat16)
    grad_in_all = lax.all_gather(grad_in, "gene", axis=0, tiled=True)
    gene_grad = contract_cols(grad_in_all, enc_weight).astype(jnp.bfloat16)
    enc_part = contract_rows(gene_counts, grad_in_all)
    enc_grad, dec_grad = (
        lax.psum_scatter(enc_part, "dp", scatter_dimension=1, tiled=True),
        lax.psum_scatter(dec_part, "dp", scatter_dimension=0, tiled=True),
    )
    attn_part = jnp.concatenate([proj_part, out_part], axis=0)
    gain_part = jnp.concatenate([gain_first, gain_second], axis=0)
    attn_grad, up_grad, down_grad, gain_grad, bias_grad, mid_bias_grad = (
        lax.psum_scatter(attn_part, ("dp", "gene"), scatter_dimension=0, tiled=True),
        lax.psum_scatter(up_part, ("dp", "gene"), scatter_dimension=0, tiled=True),
        lax.psum_scatter(down_part, ("dp", "gene"), scatter_dimension=0, tiled=True),
        lax.psum_scatter(gain_part, ("dp", "gene"), scatter_dimension=0, tiled=True),
        lax.psum_scatter(bias_first, ("dp", "gene"), scatter_dimension=0, tiled=True),
        lax.psum_scatter(bias_second, ("dp", "gene"), scatter_dimension=0, tiled=True),
    )
    return (
        logits,
        gene_grad,
        enc_grad,
        dec_grad,
        attn_grad,
        up_grad,
        down_grad,
        gain_grad,
        bias_grad,
        mid_bias_grad,
    )


def solution(mesh):
    in_specs = (
        P("dp", "gene"),
        P(None, ("dp", "gene")),
        P("dp", None),
        P("gene", None),
        P(None, "gene"),
        P(("dp", "gene"), None),
        P(("dp", "gene"), None),
        P(("dp", "gene"), None),
        P(("dp", "gene")),
        P(("dp", "gene")),
        P("dp", "gene"),
    )
    out_specs = (
        P("dp", "gene"),
        P("dp", "gene"),
        P("gene", "dp"),
        P("dp", "gene"),
        P(("dp", "gene"), None),
        P(("dp", "gene"), None),
        P(("dp", "gene"), None),
        P(("dp", "gene")),
        P(("dp", "gene")),
        P(("dp", "gene")),
    )
    return jax.shard_map(body, mesh=mesh, in_specs=in_specs, out_specs=out_specs, check_vma=False)
```

profile of v0, /device:TPU:0, one launch (start us, length us, event | category | flops | bytes accessed | tf_op | source)
XLA Modules:
  0.0 1780.0 jit_solution(872594168447583471)
XLA Ops:
  10.0 7.9 convolution_convert_fusion.2
  21.6 9.0 fusion.29
  31.8 42.7 %all-reduce.6 = (bf16[2048]{0:T(1024)(128)(2,1)S(1)}, bf16[2048]{0:T(1024)(128)(2,1)S(1)}) all-reduce(bf16[2048]{0:T(1024)(128)(2,1)S(1)} %dynamic-update-slice.1, bf16[2048]{0:T(1024)(128)(2,1)S(1)} %dynamic-update-slice), channel_id=1, replica_groups=mesh['dp'=8,'gene'=4] {'dp','gene'}, use_global_device_ids=true, to_apply=%add.1 | all-reduce | flops 4096 | bytes 16384
  78.7 41.6 %all-gather.7.cloned.1.call-done = bf16[4096,1024]{1,0:T(8,128)(2,1)} async-done(((bf16[128,1024]{1,0:T(8,128)(2,1)}), bf16[4096,1024]{1,0:T(8,128)(2,1)}) %all-gather.7.cloned.1.call-update) | async-done | bytes 8388624 | tf_op jit(solution)/shard_map/all_gather | solution.py:80
  120.3 5.2 fusion.5
  132.4 66.7 %all-gather.13.cloned.1.call-done = bf16[4096,1024]{1,0:T(8,128)(2,1)} async-done(((bf16[128,1024]{1,0:T(8,128)(2,1)}), bf16[4096,1024]{1,0:T(8,128)(2,1)}) %all-gather.13.cloned.1.call-update) | async-done | bytes 8388624 | tf_op jit(solution)/shard_map/all_gather | solution.py:82
  199.1 7.7 fusion.65
  206.8 38.6 %all-gather.9.cloned.1.call-done = bf16[512,2048]{1,0:T(8,128)(2,1)} async-done(((bf16[128,2048]{1,0:T(8,128)(2,1)}), bf16[512,2048]{1,0:T(8,128)(2,1)}) %all-gather.9.cloned.1.call-update) | async-done | bytes 2097168 | tf_op jit(solution)/shard_map/all_gather | solution.py:103
  253.1 4.8 fusion.63
  257.9 3.5 convolution_convert_fusion.3
  264.7 59.8 %all-gather.11.cloned.1.call-done = bf16[4096,1024]{1,0:T(8,128)(2,1)} async-done(((bf16[128,1024]{1,0:T(8,128)(2,1)}), bf16[4096,1024]{1,0:T(8,128)(2,1)}) %all-gather.11.cloned.1.call-update) | async-done | bytes 8388624 | tf_op jit(solution)/shard_map/all_gather | solution.py:81
  324.5 9.6 fusion.19
  351.4 4.0 copy.37
  355.9 6.3 fusion.35
  362.2 3.5 fusion.36
  365.7 32.4 %reduce-scatter.25.cloned.1.call-done = bf16[128,2048]{1,0:T(8,128)(2,1)} async-done(((bf16[512,2048]{1,0:T(8,128)(2,1)}), bf16[128,2048]{1,0:T(8,128)(2,1)}) %reduce-scatter.25.cloned.1.call-update) | async-done | bytes 524304
  400.1 4.3 multiply_reduce_fusion.2
  405.7 21.7 %all-gather.15.cloned.1.call-done = bf16[512,1024]{1,0:T(8,128)(2,1)} async-done(((bf16[128,1024]{1,0:T(8,128)(2,1)}), bf16[512,1024]{1,0:T(8,128)(2,1)}) %all-gather.15.cloned.1.call-update) | async-done | bytes 1048592 | tf_op jit(solution)/shard_map/all_gather | solution.py:128
  427.4 11.0 fusion.9
  438.5 18.5 %all-gather.17.cloned.1.call-done = bf16[512,1024]{1,0:T(8,128)(2,1)} async-done(((bf16[128,1024]{1,0:T(8,128)(2,1)}), bf16[512,1024]{1,0:T(8,128)(2,1)}) %all-gather.17.cloned.1.call-update) | async-done | bytes 1048592 | tf_op jit(solution)/shard_map/all_gather | solution.py:181
  457.0 8.1 convolution_bitcast_fusion
  467.3 11.3 fusion.55
  480.6 8.6 fusion.53
  492.8 7.2 pad_maximum_fusion
  501.2 8.2 multiply_convert_fusion
  509.4 39.9 %all-reduce.5 = (f32[2048]{0:T(1024)S(1)}, f32[1024]{0:T(1024)S(1)}, f32[1024]{0:T(1024)S(1)}) all-reduce(f32[2048]{0:T(1024)S(1)} %pad_maximum_fusion.5, f32[1024]{0:T(1024)S(1)} %get-tuple-element.15, f32[1024]{0:T(1024)S(1)} %get-tuple-element.14), channel_id=10, replica_groups=mesh['dp'=8,'gene'=4] {'dp','gene'}, use_global_device_ids=true, to_apply=%region_21.22.clone | all-reduce | flops 4096 | bytes 32768
  551.1 9.0 convolution_convert_fusion
  560.1 6.1 reduce-scatter.17.cloned.1.call-done
  566.2 108.6 %reduce-scatter.15.cloned.1.call-done = f32[3375,128]{1,0:T(8,128)} async-done(((f32[3375,1024]{1,0:T(8,128)}), f32[3375,128]{1,0:T(8,128)}) %reduce-scatter.15.cloned.1.call-update) | async-done | bytes 1728016 | tf_op jit(solution)/shard_map/reduce_scatter | solution.py:185
  674.8 367.2 %reduce-scatter.23.cloned.1.call-done = f32[128,1024]{1,0:T(8,128)} async-done(((f32[4096,1024]{1,0:T(8,128)}), f32[128,1024]{1,0:T(8,128)}) %reduce-scatter.23.cloned.1.call-update) | async-done | bytes 524304 | tf_op jit(solution)/shard_map/reduce_scatter | solution.py:193
  1042.0 365.2 %reduce-scatter.21.cloned.1.call-done = f32[128,1024]{1,0:T(8,128)} async-done(((f32[4096,1024]{1,0:T(8,128)}), f32[128,1024]{1,0:T(8,128)}) %reduce-scatter.21.cloned.1.call-update) | async-done | bytes 524304 | tf_op jit(solution)/shard_map/reduce_scatter | solution.py:192
  1407.1 365.0 %reduce-scatter.19.cloned.1.call-done = f32[128,1024]{1,0:T(8,128)} async-done(((f32[4096,1024]{1,0:T(8,128)}), f32[128,1024]{1,0:T(8,128)}) %reduce-scatter.19.cloned.1.call-update) | async-done | bytes 524304 | tf_op jit(solution)/shard_map/reduce_scatter | solution.py:191
  (159 shorter events, 59.2 us)
Async XLA Ops:
  8.0 68.3 %reduce-scatter.11.cloned.1.call-start = ((), (), s32[]{:S(2)}) async-start(), calls=%async_computation.8 | async-start | bytes 1310720 | tf_op jit(solution)/shard_map/reduce_scatter | solution.py:90
  10.0 8.6 copy-start.30
  17.9 102.4 %all-gather.7.cloned.1.call-start = ((), (), s32[]{:S(2)}) async-start(), calls=%async_computation.9 | async-start | bytes 8650752 | tf_op jit(solution)/shard_map/all_gather | solution.py:80
  18.5 113.9 %reduce-scatter.13.cloned.1.call-start = ((), (), s32[]{:S(2)}) async-start(), calls=%async_computation.14 | async-start | bytes 1310720 | tf_op jit(solution)/shard_map/reduce_scatter | solution.py:132
  21.6 9.7 copy-start.37
  21.6 9.9 copy-start.38
  21.6 52.9 %copy-start.31 = (f32[2,128]{1,0:T(2,128)S(1)}, f32[2,128]{1,0:T(2,128)}, u32[]{:S(2)}) copy-start(f32[2,128]{1,0:T(2,128)} %param.12) | copy-start | bytes 3076
  30.6 168.5 %all-gather.13.cloned.1.call-start = ((), (), s32[]{:S(2)}) async-start(), calls=%async_computation.12 | async-start | bytes 8650752 | tf_op jit(solution)/shard_map/all_gather | solution.py:82
  31.2 214.1 %all-gather.9.cloned.1.call-start = ((), (), s32[]{:S(2)}) async-start(), calls=%async_computation.10 | async-start | bytes 2621440 | tf_op jit(solution)/shard_map/all_gather | solution.py:103
  78.7 46.9 %copy-start.34 = (f32[128]{0:T(128)}, f32[128]{0:T(128)S(1)}, u32[]{:S(2)}) copy-start(f32[128]{0:T(128)S(1)} %multiply_reduce_fusion.6) | copy-start | bytes 1540
  127.3 197.2 %all-gather.11.cloned.1.call-start = ((), (), s32[]{:S(2)}) async-start(), calls=%async_computation.11 | async-start | bytes 8650752 | tf_op jit(solution)/shard_map/all_gather | solution.py:81
  128.0 270.0 %reduce-scatter.25.cloned.1.call-start = ((), (), s32[]{:S(2)}) async-start(), calls=%async_computation.21 | async-start | bytes 2621440
  257.9 3.5 copy-start.5
  261.4 3.3 copy-start.22
  324.5 9.6 copy-start.2
  324.5 9.6 copy-start.9
  342.4 3.5 copy-start.15
  342.4 3.8 copy-start.24
  342.4 3.9 copy-start.29
  355.4 72.0 %all-gather.15.cloned.1.call-start = ((), (), s32[]{:S(2)}) async-start(), calls=%async_computation.13 | async-start | bytes 1310720 | tf_op jit(solution)/shard_map/all_gather | solution.py:128
  362.2 94.8 %all-gather.17.cloned.1.call-start = ((), (), s32[]{:S(2)}) async-start(), calls=%async_computation.15 | async-start | bytes 1310720 | tf_op jit(solution)/shard_map/all_gather | solution.py:181
  400.1 4.4 copy-start.35
  400.1 4.4 copy-start.6
  400.1 4.7 copy-start.14
  400.1 4.7 copy-start.17
  400.1 27.3 %copy-start.33 = (bf16[512]{0:T(512)(128)(2,1)S(1)}, bf16[512]{0:T(512)(128)(2,1)}, u32[]{:S(2)}) copy-start(bf16[512]{0:T(512)(128)(2,1)} %copy-done.32) | copy-start | bytes 3076
  405.7 160.5 %reduce-scatter.17.cloned.1.call-start = ((), (), s32[]{:S(2)}) async-start(), calls=%async_computation.17 | async-start | bytes 15556608 | tf_op jit(solution)/shard_map/reduce_scatter | solution.py:186
  438.4 236.3 %reduce-scatter.15.cloned.1.call-start = ((), (), s32[]{:S(2)}) async-start(), calls=%async_computation.16 | async-start | bytes 15556608 | tf_op jit(solution)/shard_map/reduce_scatter | solution.py:185
  465.1 576.8 %reduce-scatter.23.cloned.1.call-start = ((), (), s32[]{:S(2)}) async-start(), calls=%async_computation.20 | async-start | bytes 17301504 | tf_op jit(solution)/shard_map/reduce_scatter | solution.py:193
  478.7 928.5 %reduce-scatter.21.cloned.1.call-start = ((), (), s32[]{:S(2)}) async-start(), calls=%async_computation.19 | async-start | bytes 17301504 | tf_op jit(solution)/shard_map/reduce_scatter | solution.py:192
  489.2 1282.9 %reduce-scatter.19.cloned.1.call-start = ((), (), s32[]{:S(2)}) async-start(), calls=%async_computation.18 | async-start | bytes 17301504 | tf_op jit(solution)/shard_map/reduce_scatter | solution.py:191
  551.1 1221.1 %copy-start.1 = (bf16[512,3375]{0,1:T(8,128)(2,1)S(1)}, bf16[512,3375]{0,1:T(8,128)(2,1)}, u32[]{:S(2)}) copy-start(bf16[512,3375]{0,1:T(8,128)(2,1)} %param.11) | copy-start | bytes 10368004
  (21 other events, 28.5 us)
Sparse Core Ops, SparseCore 0:
  18.1 33.6 reduce-scatter.10
  54.7 36.3 reduce-scatter.12
  355.5 42.4 reduce-scatter.24
  400.1 27.2 all-gather.14
  429.5 27.4 all-gather.16
  461.4 104.7 reduce-scatter.16
  570.7 103.9 reduce-scatter.14
  677.7 364.1 reduce-scatter.22
  1044.9 362.1 reduce-scatter.20
  1410.0 362.1 reduce-scatter.18
Sparse Core Ops, SparseCore 1:
  21.3 98.9 all-gather.6
  123.1 75.9 all-gather.12
  201.1 44.2 all-gather.8
  248.3 76.1 all-gather.10
where the time goes:
time: 1790 us; the launch traced here: 1780 us
  waiting for transfers between devices  1490 us (83%)
  matrix products  132 us (7%)
  blocking collectives  82.6 us (5%)
  local copies, waits for them, and re-layouts  36.7 us (2%)
    reduce_scatter x1, waiting for transfers between devices, body(): lax.psum_scatter(down_part, ('dp', 'gene'), scatter_dimension=0, tiled=True)  367 us
    reduce_scatter x1, waiting for transfers between devices, body(): lax.psum_scatter(up_part, ('dp', 'gene'), scatter_dimension=0, tiled=True)  365 us
    reduce_scatter x1, waiting for transfers between devices, body(): lax.psum_scatter(attn_part, ('dp', 'gene'), scatter_dimension=0, tiled=True)  365 us
    reduce_scatter x1, waiting for transfers between devices, body(): lax.psum_scatter(enc_part, 'dp', scatter_dimension=1, tiled=True)  109 us
    unnamed x2, blocking collectives  82.6 us
    all_gather x1, waiting for transfers between devices, body(): lax.all_gather(down_weight, ('dp', 'gene'), axis=0, tiled=True)  66.7 us
    all_gather x1, waiting for transfers between devices, body(): lax.all_gather(up_weight, ('dp', 'gene'), axis=0, tiled=True)  59.8 us
    dot_general x6, matrix products, contract_cols(): lax.dot_general(left, right, (((1,), (1,)), ((), ())), preferred_element_...  43.5 us
  transfers between devices with their start and end apart: 14, of which 12 were waited for; matrix products, arithmetic and copies ran while one was open for 8% of the time, Pallas kernels for 0%

commit v1 on v0

--- a/solution.py
+++ b/solution.py
@@ -1,8 +1,11 @@
+import functools
 import math
 
 import jax
 import jax.numpy as jnp
 from jax import lax
+from jax.experimental import pallas as pl
+from jax.experimental.pallas import tpu as pltpu
 from jax.sharding import PartitionSpec as P
 
 HEADS = 16
@@ -209,7 +212,517 @@
     )
 
 
+MESH = pl.DeviceIdType.MESH
+MIB = 2**20
+VMEM = pl.BlockSpec(memory_space=pltpu.VMEM)
+SMEM = pl.BlockSpec(memory_space=pltpu.SMEM)
+ANY = pl.BlockSpec(memory_space=pl.ANY)
+DMA = pltpu.SemaphoreType.DMA
+
+
+class Place:
+    def __init__(self):
+        self.dp = dp = lax.axis_index("dp")
+        self.z = z = lax.axis_index("gene")
+        self.core = dp % 2
+        self.chip = dp // 2
+        self.inner = z * (3 - z) > 0
+        self.outer = z * (3 - z) == 0
+        self.pair = (dp, z + 1 - 2 * (z % 2))
+        self.middle = (dp, 3 - z)
+        self.sibling_dp = dp + 1 - 2 * (dp % 2)
+        self.x_dp = dp + 2 - 4 * ((dp // 2) % 2)
+        self.y_dp = dp + 4 - 8 * (dp // 4)
+        self.xy_dp = self.x_dp + 4 - 8 * (dp // 4)
+        self.sibling = (self.sibling_dp, z)
+        self.far_dps = (self.x_dp, self.y_dp, self.xy_dp)
+        self.far = tuple((d, z) for d in self.far_dps)
+        self.line = tuple((dp, (z + k) % 4) for k in (1, 2, 3))
+
+    def meet(self, devices):
+        barrier = pltpu.get_barrier_semaphore()
+        for device in devices:
+            pl.semaphore_signal(barrier, inc=1, device_id=device, device_id_type=MESH)
+        pl.semaphore_wait(barrier, len(devices))
+
+    def meet_line(self):
+        barrier = pltpu.get_barrier_semaphore()
+        pl.semaphore_signal(barrier, inc=1, device_id=self.pair, device_id_type=MESH)
+
+        @pl.when(self.inner)
+        def _():
+            pl.semaphore_signal(barrier, inc=1, device_id=self.middle, device_id_type=MESH)
+            pl.semaphore_wait(barrier, 2)
+
+        @pl.when(self.outer)
+        def _():
+            pl.semaphore_wait(barrier, 1)
+
+
+def send(src, dst, send_sem, recv_sem, device):
+    return pltpu.make_async_remote_copy(
+        src_ref=src,
+        dst_ref=dst,
+        send_sem=send_sem,
+        recv_sem=recv_sem,
+        device_id=device,
+        device_id_type=MESH,
+    )
+
+
+class LineSum:
+    SEMS = 6
+
+    def __init__(self, place, part, inbox, peer, total, sems, view):
+        self.place, self.part, self.inbox, self.peer, self.total = place, part, inbox, peer, total
+        self.sems, self.view = sems, view
+
+    def up(self, k):
+        s, v = self.sems, self.view
+        return send(v(self.part, k), v(self.inbox, k), s.at[0, k], s.at[1, k], self.place.pair)
+
+    def across(self, k):
+        s, v = self.sems, self.view
+        return send(v(self.part, k), v(self.peer, k), s.at[2, k], s.at[3, k], self.place.middle)
+
+    def down(self, k):
+        s, v = self.sems, self.view
+        return send(v(self.total, k), v(self.total, k), s.at[4, k], s.at[5, k], self.place.pair)
+
+    def push(self, k):
+        @pl.when(self.place.outer)
+        def _():
+            self.up(k).start()
+
+    def meet_up(self, k):
+        @pl.when(self.place.inner)
+        def _():
+            self.up(k).wait_recv()
+            mine, other = self.view(self.part, k), self.view(self.inbox, k)
+            mine[...] = (mine[...].astype(jnp.float32) + other[...].astype(jnp.float32)).astype(
+                jnp.bfloat16
+            )
+            self.across(k).start()
+
+    def meet_across(self, k):
+        @pl.when(self.place.inner)
+        def _():
+            self.across(k).wait_recv()
+            mine, other = self.view(self.part, k), self.view(self.peer, k)
+            self.view(self.total, k)[...] = (
+                mine[...].astype(jnp.float32) + other[...].astype(jnp.float32)
+            ).astype(jnp.bfloat16)
+            self.down(k).start()
+
+    def get(self, k):
+        @pl.when(self.place.outer)
+        def _():
+            self.down(k).wait_recv()
+
+    def finish(self, count):
+        @pl.when(self.place.outer)
+        def _():
+            for k in range(count):
+                self.up(k).wait_send()
+
+        @pl.when(self.place.inner)
+        def _():
+            for k in range(count):
+                self.across(k).wait_send()
+                self.down(k).wait_send()
+
+
+def chunk(ref, k):
+    return ref.at[k]
+
+
+def columns(ref, k, width):
+    return ref.at[:, pl.ds(k * width, width)]
+
+
+def row_live(lengths, rows):
+    index = lax.broadcasted_iota(jnp.int32, (rows, 1), 0)
+    return (index < lengths[0, 0] + lengths[0, 1]).astype(jnp.float32)
+
+
+def encode_kernel(
+    coords,
+    lengths,
+    counts,
+    enc,
+    grads,
+    dec,
+    attn,
+    up,
+    down,
+    gain,
+    bias,
+    stream,
+    grad_out,
+    weights,
+    vectors,
+    counts_v,
+    enc_v,
+    grads_v,
+    dec_v,
+    work,
+    places,
+    part_a,
+    inbox_a,
+    peer_a,
+    part_b,
+    inbox_b,
+    peer_b,
+    load_sems,
+    sems_a,
+    sems_b,
+    far_sems,
+    side_sems,
+    line_sems,
+):
+    place = Place()
+    dp, z = place.dp, place.z
+    chunks, rows, lanes = stream.shape
+    width = chunks * lanes
+    step = width // 4
+    loads = [pltpu.make_async_copy(counts, counts_v, load_sems.at[0])]
+    for j in range(4):
+        loads.append(
+            pltpu.make_async_copy(
+                columns(enc, j, step), columns(enc_v, j, step), load_sems.at[1 + j]
+            )
+        )
+    loads.append(pltpu.make_async_copy(grads, grads_v, load_sems.at[5]))
+    for j in range(4):
+        loads.append(
+            pltpu.make_async_copy(
+                columns(dec, j, step), columns(dec_v, j, step), load_sems.at[6 + j]
+            )
+        )
+    for copy in loads:
+        copy.start()
+    for i, ref in enumerate((attn, up, down)):
+        weights[i, dp] = ref[...]
+    place.meet(place.far + (place.sibling,) + place.line)
+
+    tile = vectors.at[dp * 4 + z]
+    tile[...] = jnp.zeros_like(tile)
+    tile[0:1, 0:64] = gain[...].astype(jnp.float32)
+    tile[1:2, 0:64] = bias[...].astype(jnp.float32)
+    line_out = [
+        send(tile, tile, line_sems.at[0, i], line_sems.at[1, i], device)
+        for i, device in enumerate(place.line)
+    ]
+    for copy in line_out:
+        copy.start()
+
+    def block_of(d):
+        return weights.at[:, d]
+
+    far_out = [
+        send(block_of(dp), block_of(dp), far_sems.at[0, i], far_sems.at[1, i], device)
+        for i, device in enumerate(place.far)
+    ]
+    far_in = [
+        send(block_of(d), block_of(d), far_sems.at[0, i], far_sems.at[1, i], device)
+        for i, (d, device) in enumerate(zip(place.far_dps, place.far))
+    ]
+    side_from = (dp,) + place.far_dps
+    side = [
+        send(block_of(d), block_of(d), side_sems.at[0, i], side_sems.at[1, i], place.sibling)
+        for i, d in enumerate(side_from)
+    ]
+    for copy in far_out:
+        copy.start()
+    side[0].start()
+
+    def lines(d):
+        return vectors.at[pl.ds(d * 4, 4)]
+
+    vec_far = [
+        send(lines(dp), lines(dp), far_sems.at[2, i], far_sems.at[3, i], device)
+        for i, device in enumerate(place.far)
+    ]
+    vec_side = [
+        send(lines(d), lines(d), side_sems.at[2, i], side_sems.at[3, i], place.sibling)
+        for i, d in enumerate(side_from)
+    ]
+
+    own_rows = coords.shape[1]
+    index = lax.broadcasted_iota(jnp.int32, (1, step), 1).astype(jnp.float32)
+    freqs = jnp.exp(index * (-4.0 * math.log(10000.0) / width))
+    for axis in range(2):
+        along = jnp.broadcast_to(coords[axis : axis + 1, :], (own_rows, own_rows)).T
+        angle = along[:, 0:1] * freqs
+        places[2 * axis] = jnp.sin(angle)
+        places[2 * axis + 1] = jnp.cos(angle)
+
+    sum_a = LineSum(place, part_a, inbox_a, peer_a, stream, sems_a, chunk)
+    sum_b = LineSum(place, part_b, inbox_b, peer_b, grad_out, sems_b, chunk)
+    live = row_live(lengths, rows)
+    own = pl.ds(pl.multiple_of(z * own_rows, own_rows), own_rows)
+    per = step // lanes
+
+    def encode(j):
+        if j == 0:
+            loads[0].wait()
+        loads[1 + j].wait()
+        work[...] = contract_rows(counts_v[...], enc_v[:, j * step : (j + 1) * step])
+        work[own, :] += places[j]
+        for k in range(per):
+            part_a[j * per + k] = work[:, k * lanes : (k + 1) * lanes].astype(jnp.bfloat16)
+            sum_a.push(j * per + k)
+
+    def decode(j):
+        if j == 0:
+            loads[5].wait()
+        loads[6 + j].wait()
+        got = contract_rows(grads_v[...], dec_v[:, j * step : (j + 1) * step]) * live
+        for k in range(per):
+            part_b[j * per + k] = got[:, k * lanes : (k + 1) * lanes].astype(jnp.bfloat16)
+            sum_b.push(j * per + k)
+
+    produce = [functools.partial(encode, j) for j in range(4)]
+    produce += [functools.partial(decode, j) for j in range(4)]
+    ups = [functools.partial(sum_a.meet_up, k) for k in range(8)]
+    ups += [functools.partial(sum_b.meet_up, k) for k in range(8)]
+    acrosses = [functools.partial(sum_a.meet_across, k) for k in range(8)]
+    acrosses += [functools.partial(sum_b.meet_across, k) for k in range(8)]
+
+    def vectors_out():
+        for copy in line_out:
+            copy.wait_recv()
+        for copy in vec_far + vec_side[:1]:
+            copy.start()
+
+    def weights_on():
+        for i in range(3):
+            far_in[i].wait_recv()
+            side[1 + i].start()
+            vec_far[i].wait_recv()
+            vec_side[1 + i].start()
+
+    made = 0
+    for k in range(17):
+        while made < 8 and made * per < k + per + 2:
+            produce[made]()
+            made += 1
+        if k < 16:
+            ups[k]()
+        if k == 4:
+            vectors_out()
+        if k == 13:
+            weights_on()
+        if k >= 1:
+            acrosses[k - 1]()
+    for k in range(8):
+        sum_a.get(k)
+    for k in range(8):
+        sum_b.get(k)
+    sum_a.finish(8)
+    sum_b.finish(8)
+    for copy in line_out:
+        copy.wait_send()
+    for copy in far_out + vec_far:
+        copy.wait_send()
+    for copy in side + vec_side:
+        copy.wait()
+
+
+def encode_call(coords, lengths, counts, enc, grads, dec, attn, up, down, gain, bias):
+    genes, rows = counts.shape
+    width = enc.shape[1]
+    low, full = jnp.bfloat16, jnp.float32
+    block = pltpu.VMEM((width // 128, rows, 128), low)
+    return pl.pallas_call(
+        encode_kernel,
+        out_shape=(
+            jax.ShapeDtypeStruct((width // 128, rows, 128), low),
+            jax.ShapeDtypeStruct((width // 128, rows, 128), low),
+            jax.ShapeDtypeStruct((3, 8) + attn.shape, low),
+            jax.ShapeDtypeStruct((32, 8, 128), full),
+        ),
+        in_specs=[VMEM, SMEM, ANY, ANY, ANY, ANY, VMEM, VMEM, VMEM, VMEM, VMEM],
+        out_specs=(VMEM, VMEM, VMEM, VMEM),
+        scratch_shapes=[
+            pltpu.VMEM((genes, rows), low),
+            pltpu.VMEM((genes, width), low),
+            pltpu.VMEM((genes, rows), low),
+            pltpu.VMEM((genes, width), low),
+            pltpu.VMEM((rows, width // 4), full),
+            pltpu.VMEM((4, coords.shape[1], width // 4), full),
+            block,
+            block,
+            block,
+            block,
+            block,
+            block,
+            DMA((10,)),
+            DMA((6, 8)),
+            DMA((6, 8)),
+            DMA((4, 3)),
+            DMA((4, 4)),
+            DMA((2, 3)),
+        ],
+        compiler_params=pltpu.CompilerParams(
+            collective_id=0, has_side_effects=True, vmem_limit_bytes=56 * MIB
+        ),
+        name="encode",
+    )(coords, lengths, counts, enc, grads, dec, attn, up, down, gain, bias)
+
+
+def fast_body(
+    gene_counts,
+    coords,
+    lengths,
+    enc_weight,
+    dec_weight,
+    attn_weight,
+    up_weight,
+    down_weight,
+    ln_gain,
+    ln_bias,
+    logit_grad,
+):
+    model_width = enc_weight.shape[1]
+    group_rows = gene_counts.shape[0]
+    local = model_width // 4
+    heads = HEADS // 4
+    score_scale = 1.0 / math.sqrt(HEAD_DIM)
+    slide = slide_ids(lengths[0], group_rows)
+    live = (slide < 2).astype(jnp.bfloat16)[:, None]
+    stream_in, grad_out, weights, vectors = encode_call(
+        coords,
+        lengths,
+        gene_counts.T,
+        enc_weight,
+        logit_grad.T,
+        dec_weight.T,
+        attn_weight,
+        up_weight,
+        down_weight,
+        ln_gain[None],
+        ln_bias[None],
+    )
+    norm_gains = vectors[:, 0, :64].reshape(2 * model_width)
+    offsets = vectors[:, 1, :64].reshape(2 * model_width)
+    attn_full, up_full, down_full = [weights[i].reshape(-1, model_width) for i in range(3)]
+    proj_weight, out_weight = attn_full[: 3 * local], attn_full[3 * local :]
+
+    def sum_line(part):
+        return lax.psum(part.astype(jnp.bfloat16), "gene").astype(jnp.float32)
+
+    stream_in, grad_out = [
+        jnp.swapaxes(v, 0, 1).reshape(group_rows, model_width).astype(jnp.float32)
+        for v in (stream_in, grad_out)
+    ]
+    first_normed, first_pull = jax.vjp(
+        norm_rows, stream_in, norm_gains[:model_width], offsets[:model_width]
+    )
+    first_low = first_normed.astype(jnp.bfloat16)
+    projected = contract_cols(first_low, proj_weight).astype(jnp.bfloat16)
+    queries, keys, values = [
+        projected[:, i * local : (i + 1) * local].reshape(group_rows, heads, HEAD_DIM)
+        for i in range(3)
+    ]
+    same_slide = (slide[:, None] == slide[None, :])[None]
+    scores = (
+        jnp.einsum("qhd,khd->hqk", queries, keys, preferred_element_type=jnp.float32)
+        * score_scale
+    )
+    scores = jnp.where(same_slide, scores, -1e30)
+    row_max = jnp.max(scores, axis=-1, keepdims=True)
+    raised = jnp.exp(scores - row_max)
+    soft = raised / jnp.sum(raised, axis=-1, keepdims=True)
+    soft_low = soft.astype(jnp.bfloat16)
+    attended = jnp.einsum("hqk,khd->qhd", soft_low, values, preferred_element_type=jnp.float32)
+    attended = attended.reshape(group_rows, local).astype(jnp.bfloat16)
+    stream_mid = stream_in + sum_line(product(attended, out_weight))
+    second_normed, second_pull = jax.vjp(
+        norm_rows, stream_mid, norm_gains[model_width:], offsets[model_width:]
+    )
+    second_low = second_normed.astype(jnp.bfloat16)
+    hidden_pre = contract_cols(second_low, up_full)
+    active, gelu_pull = jax.vjp(gelu_tanh, hidden_pre)
+    active_low = active.astype(jnp.bfloat16)
+    stream_out = stream_mid + sum_line(product(active_low, down_full))
+    cells = stream_out.astype(jnp.bfloat16) * live
+    logits = product(cells, dec_weight).astype(jnp.bfloat16)
+    dec_part = contract_rows(cells, logit_grad).astype(jnp.bfloat16)
+    dec_grad = lax.psum_scatter(dec_part, "dp", scatter_dimension=0, tiled=True)
+    grad_branch = grad_out.astype(jnp.bfloat16)
+    down_part = contract_rows(active_low, grad_branch)
+    grad_active = contract_cols(grad_branch, down_full)
+    grad_hidden = gelu_pull(grad_active)[0].astype(jnp.bfloat16)
+    up_part = contract_rows(grad_hidden, second_low)
+    grad_second = sum_line(product(grad_hidden, up_full))
+    grad_mid_norm, gain_second, bias_second = second_pull(grad_second)
+    grad_mid = grad_out + grad_mid_norm
+    grad_attn = grad_mid.astype(jnp.bfloat16)
+    out_part = contract_rows(attended, grad_attn)
+    grad_attended = (
+        contract_cols(grad_attn, out_weight)
+        .astype(jnp.bfloat16)
+        .reshape(group_rows, heads, HEAD_DIM)
+    )
+    grad_soft = jnp.einsum(
+        "qhd,khd->hqk", grad_attended, values, preferred_element_type=jnp.float32
+    )
+    grad_scores = soft * (grad_soft - jnp.sum(grad_soft * soft, axis=-1, keepdims=True))
+    grad_scores = grad_scores.astype(jnp.bfloat16)
+    grad_query = (
+        jnp.einsum("hqk,khd->qhd", grad_scores, keys, preferred_element_type=jnp.float32)
+        * score_scale
+    )
+    grad_keys = (
+        jnp.einsum("hqk,qhd->khd", grad_scores, queries, preferred_element_type=jnp.float32)
+        * score_scale
+    )
+    grad_values = jnp.einsum(
+        "hqk,qhd->khd", soft_low, grad_attended, preferred_element_type=jnp.float32
+    )
+    grad_proj = jnp.concatenate(
+        [g.reshape(group_rows, local) for g in (grad_query, grad_keys, grad_values)], axis=1
+    ).astype(jnp.bfloat16)
+    proj_part = contract_rows(grad_proj, first_low)
+    grad_first = sum_line(product(grad_proj, proj_weight))
+    grad_in_norm, gain_first, bias_first = first_pull(grad_first)
+    grad_in = (grad_mid + grad_in_norm).astype(jnp.bfloat16)
+    gene_grad = contract_cols(grad_in, enc_weight).astype(jnp.bfloat16)
+    enc_part = contract_rows(gene_counts, grad_in).astype(jnp.bfloat16)
+    enc_grad = lax.psum_scatter(enc_part, "dp", scatter_dimension=1, tiled=True)
+    layer_part = jnp.stack(
+        [
+            part.astype(jnp.bfloat16).reshape(8, -1, model_width)
+            for part in (jnp.concatenate([proj_part, out_part], axis=0), up_part, down_part)
+        ],
+        axis=1,
+    )
+    layer_grad = lax.psum_scatter(layer_part, "dp", scatter_dimension=0, tiled=True)[0]
+    small = jnp.concatenate([gain_first, gain_second, bias_first, bias_second])
+    small = lax.psum(small, "dp")
+    place = lax.axis_index("dp") * 4 + lax.axis_index("gene")
+    gain_grad = lax.dynamic_slice_in_dim(small[: 2 * model_width], place * 64, 64)
+    bias_grad = lax.dynamic_slice_in_dim(
+        small[2 * model_width : 3 * model_width], place * 32, 32
+    )
+    mid_bias_grad = lax.dynamic_slice_in_dim(small[3 * model_width :], place * 32, 32)
+    return (
+        logits,
+        gene_grad,
+        enc_grad.astype(jnp.float32),
+        dec_grad.astype(jnp.float32),
+        layer_grad[0].astype(jnp.float32),
+        layer_grad[1].astype(jnp.float32),
+        layer_grad[2].astype(jnp.float32),
+        gain_grad,
+        bias_grad,
+        mid_bias_grad,
+    )
+
+
 def solution(mesh):
+    fast = dict(mesh.shape) == {"dp": 8, "gene": 4}
     in_specs = (
         P("dp", "gene"),
         P(None, ("dp", "gene")),
@@ -235,4 +748,5 @@
         P(("dp", "gene")),
         P(("dp", "gene")),
     )
-    return jax.shard_map(body, mesh=mesh, in_specs=in_specs, out_specs=out_specs, check_vma=False)
+    return jax.shard_map(
+        fast_body if fast else body, mesh=mesh, in_specs=in_specs, out_specs=out_specs, check_vma=False)

time: 1790 us -> 539 us (0.30)
  waiting for transfers between devices: 1490 us -> 273 us
  Pallas kernels: 0 us -> 73.9 us
  matrix products: 132 us -> 61.9 us
  blocking collectives: 82.6 us -> 24.3 us
  local copies, waits for them, and re-layouts: 36.7 us -> 55.5 us
    reduce_scatter x7 -> x1, waiting for transfers between devices: 1210 us -> 0.01 us  [fast_body(): lax.psum_scatter(layer_part, 'dp', scatter_dimension=0, tiled=True)[0]]
    all_gather x6 -> x0, waiting for transfers between devices: 247 us -> none  [the longest x1 66.7 us: body(): lax.all_gather(down_weight, ('dp', 'gene'), axis=0, tiled=True)]
    psum x0 -> x3, waiting for transfers between devices: none -> 157 us  [sum_line(): return lax.psum(part.astype(jnp.bfloat16), 'gene').astype(jnp.float32)]
    unnamed x2 -> x0, blocking collectives: 82.6 us -> none
    unnamed x15 -> x8, waiting for transfers between devices: 34.3 us -> 116 us
    pallas_call x0 -> x1, Pallas kernels: none -> 73.9 us  [encode_call(): pl.pallas_call(encode_kernel, out_shape=(jax.ShapeDtypeStruct((width // 1...]
    dot_general x6 -> x5, matrix products: 43.5 us -> 18.7 us  [contract_cols(): lax.dot_general(left, right, (((1,), (1,)), ((), ())), preferred_element_...]
    psum x0 -> x1, blocking collectives: none -> 24.3 us  [fast_body(): small = lax.psum(small, 'dp')]
  transfers between devices with their start and end apart: 14 -> 6, of which waited for: 12 -> 5; matrix products, arithmetic and copies ran while one was open for 8% -> 17% of each run, Pallas kernels for 0% -> 0%
where the time goes in v1:
time: 539 us; the launch traced here: 530 us
  waiting for transfers between devices  273 us (51%)
  Pallas kernels  73.9 us (14%)
  matrix products  61.9 us (11%)
  local copies, waits for them, and re-layouts  55.5 us (10%)
  blocking collectives  24.3 us (5%)
  other arithmetic  23.4 us (4%)
  between operations  16.4 us (3%)
    psum x3, waiting for transfers between devices, sum_line(): return lax.psum(part.astype(jnp.bfloat16), 'gene').astype(jnp.float32)  157 us
    unnamed x8, waiting for transfers between devices  116 us
    pallas_call x1, Pallas kernels, encode_call(): pl.pallas_call(encode_kernel, out_shape=(jax.ShapeDtypeStruct((width // 1...  73.9 us
    unnamed x76, local copies, waits for them, and re-layouts  34.4 us
    psum x1, blocking collectives, fast_body(): small = lax.psum(small, 'dp')  24.3 us
    dot_general x5, matrix products, contract_cols(): lax.dot_general(left, right, (((1,), (1,)), ((), ())), preferred_element_...  18.7 us
    dot_general x6, matrix products, contract_rows(): lax.dot_general(left, right, (((0,), (0,)), ((), ())), preferred_element_...  18.1 us
    dot_general x5, matrix products, product(): return jnp.dot(left, right, preferred_element_type=jnp.float32)  15.9 us
  transfers between devices with their start and end apart: 6, of which 5 were waited for; matrix products, arithmetic and copies ran while one was open for 17% of the time, Pallas kernels for 0%

profile of v1, /device:TPU:0, one launch (start us, length us, event | category | flops | bytes accessed | tf_op | source)
XLA Modules:
  0.0 529.6 jit_solution(14031340089565087520)
XLA Ops:
  8.5 73.9 %encode.1 = (bf16[8,512,128]{2,1,0:T(8,128)(2,1)}, bf16[8,512,128]{2,1,0:T(8,128)(2,1)}, bf16[3,8,128,1024]{3,2,1,0:T(8,128)(2,1)}, f32[32,8,128]{2,1,0:T(8,128)}) custom-call(f32[2,128]{1,0:T(2,128)} %coords.1, s32[1,2]{1,0:T(1,128)} %lengths.1, bf16[3375,512]{1,0:T(8,128)(2,1)} %bitcast.113, bf16[3375,1024]{1,0:T(8,128)(2,1)} %enc.1, ...), custom_call_target="tpu_custom_call" | custom-call | tf_op jit(solution)/shard_map/encode/pallas_call | solution.py:537
  83.6 2.9 slice.84
  92.4 2.8 convolution_convert_fusion.11
  95.7 3.7 fusion.57
  99.4 2.7 convolution_convert_fusion.15
  107.6 2.0 copy.56
  109.6 4.1 fusion.53
  115.0 2.6 fusion.58
  117.6 37.0 %all-reduce.5.cloned.1.call-done = bf16[512,1024]{1,0:T(8,128)(2,1)} async-done(((bf16[512,1024]{1,0:T(8,128)(2,1)}), bf16[512,1024]{1,0:T(8,128)(2,1)}) %all-reduce.5.cloned.1.call-update) | async-done | bytes 1048592 | tf_op jit(solution)/shard_map/psum | solution.py:613
  156.7 2.0 copy-done.19
  158.7 3.9 fusion.21
  162.6 2.2 convolution_convert_fusion.8
  166.6 5.0 convolution_convert_fusion.9
  171.6 44.6 %all-reduce.7.cloned.1.call-done = bf16[512,1024]{1,0:T(8,128)(2,1)} async-done(((bf16[512,1024]{1,0:T(8,128)(2,1)}), bf16[512,1024]{1,0:T(8,128)(2,1)}) %all-reduce.7.cloned.1.call-update) | async-done | bytes 1048592 | tf_op jit(solution)/shard_map/psum | solution.py:613
  216.2 2.9 fusion.22
  227.7 2.0 convolution_convert_fusion.7
  230.1 3.5 convolution_convert_fusion.5
  237.0 3.3 pad_maximum_fusion
  241.0 75.4 %all-reduce.9.cloned.1.call-done = (bf16[512,1024]{1,0:T(8,128)(2,1)}, bf16[512,1024]{1,0:T(8,128)(2,1)}) async-done(((bf16[512,1024]{1,0:T(8,128)(2,1)}, bf16[512,1024]{1,0:T(8,128)(2,1)}), (bf16[512,1024]{1,0:T(8,128)(2,1)}, bf16[512,1024]{1,0:T(8,128)(2,1)})) %all-reduce.9.cloned.1.call-update) | async-done | bytes 2097168 | tf_op jit(solution)/shard_map/psum | solution.py:613
  316.4 2.3 fusion.30
  319.7 5.8 %convolution_convert_fusion = bf16[1024,3375]{0,1:T(8,128)(2,1)} fusion(bf16[512,1024]{1,0:T(8,128)(2,1)S(1)} %fusion.30, bf16[512,3375]{0,1:T(8,128)(2,1)S(1)} %copy-done.14), kind=kOutput, calls=%fused_computation.1 | convolution fusion | flops 3542400000 | bytes 11416576 | tf_op jit(solution)/shard_map/dot_general | solution.py:50
  325.5 10.5 %copy.72 = bf16[1024,3375]{1,0:T(8,128)(2,1)} copy(bf16[1024,3375]{0,1:T(8,128)(2,1)} %convolution_convert_fusion) | data formatting | bytes 13824000
  341.6 5.6 %fusion.1 = bf16[3375,1024]{1,0:T(8,128)(2,1)} fusion(bf16[512,1024]{1,0:T(8,128)(2,1)S(1)} %add_convert_fusion.1, bf16[512,3375]{0,1:T(8,128)(2,1)S(1)} %copy-done.15), kind=kOutput, calls=%fused_computation.3 | convolution fusion | flops 3542400000 | bytes 11416576 | tf_op jit(solution)/shard_map/dot_general | solution.py:50
  347.2 9.9 %copy.70 = bf16[3375,1024]{0,1:T(8,128)(2,1)} copy(bf16[3375,1024]{1,0:T(8,128)(2,1)} %fusion.1) | data formatting | bytes 13824000
  357.2 24.3 %psum.39 = f32[4096]{0:T(1024)S(1)} all-reduce(f32[4096]{0:T(1024)S(1)} %pad_maximum_fusion.5), channel_id=1, replica_groups=mesh['dp'=8,'gene'=4] {'dp'}, use_global_device_ids=true, to_apply=%region_22.23 | all-reduce | flops 4096 | bytes 32768 | tf_op jit(solution)/shard_map/psum | solution.py:703
  383.3 9.0 %convolution_convert_fusion.2 = bf16[512,3375]{0,1:T(8,128)(2,1)} fusion(bf16[512,1024]{1,0:T(8,128)(2,1)} %copy-done.28, bf16[3375,1024]{1,0:T(8,128)(2,1)} %enc.1), kind=kOutput, calls=%fused_computation.5 | convolution fusion | flops 3540672000 | bytes 11416576 | tf_op jit(solution)/shard_map/dot_general | solution.py:56
  392.3 5.3 convolution_convert_fusion.3
  397.6 2.4 fusion.40
  400.0 49.9 %reduce-scatter.12.cloned.1.call-done = bf16[128,3375]{1,0:T(8,128)(2,1)} async-done(((bf16[1024,3375]{1,0:T(8,128)(2,1)}), bf16[128,3375]{1,0:T(8,128)(2,1)}) %reduce-scatter.12.cloned.1.call-update) | async-done | bytes 864016
  449.9 1.8 copy.73
  453.0 66.2 %reduce-scatter.10.cloned.1.call-done = bf16[128,3375]{1,0:T(8,128)(2,1)} async-done(((bf16[1024,3375]{1,0:T(8,128)(2,1)}), bf16[128,3375]{1,0:T(8,128)(2,1)}) %reduce-scatter.10.cloned.1.call-update) | async-done | bytes 864016
  519.2 1.8 copy.71
  (143 shorter events, 41.9 us)
Async XLA Ops:
  7.2 147.4 %all-reduce.5.cloned.1.call-start = ((), (), s32[]{:S(2)}) async-start(), calls=%async_computation.3 | async-start | bytes 2097152 | tf_op jit(solution)/shard_map/psum | solution.py:613
  82.4 7.4 %copy-start.4 = (bf16[8,512,128]{2,1,0:T(8,128)(2,1)S(1)}, bf16[8,512,128]{2,1,0:T(8,128)(2,1)}, u32[]{:S(2)}) copy-start(bf16[8,512,128]{2,1,0:T(8,128)(2,1)} %get-tuple-element.14) | copy-start | bytes 3145732
  83.6 18.5 %copy-start.16 = (bf16[1,2,128,1024]{3,2,1,0:T(8,128)(2,1)}, bf16[1,2,128,1024]{3,2,1,0:T(8,128)(2,1)S(1)}, u32[]{:S(2)}) copy-start(bf16[1,2,128,1024]{3,2,1,0:T(8,128)(2,1)S(1)} %slice.91) | copy-start | bytes 1572868
  95.4 4.0 copy-start.23
  95.5 3.9 copy-start.25
  95.7 3.7 copy-start.29
  102.1 2.1 copy-start.27
  103.6 112.6 %all-reduce.7.cloned.1.call-start = ((), (), s32[]{:S(2)}) async-start(), calls=%async_computation.4 | async-start | bytes 2097152 | tf_op jit(solution)/shard_map/psum | solution.py:613
  109.6 5.5 %copy-start.9 = (bf16[512,8,128]{0,2,1:T(8,128)(2,1)S(1)}, bf16[512,8,128]{0,2,1:T(8,128)(2,1)}, u32[]{:S(2)}) copy-start(bf16[512,8,128]{0,2,1:T(8,128)(2,1)} %copy.57) | copy-start | bytes 3145732
  154.6 2.0 copy-start.31
  156.3 6.3 %copy-start = (f32[512,1024]{1,0:T(8,128)}, f32[512,1024]{1,0:T(8,128)S(1)}, u32[]{:S(2)}) copy-start(f32[512,1024]{1,0:T(8,128)S(1)} %get-tuple-element.33) | copy-start | bytes 6291460
  156.3 2.4 copy-start.19
  162.6 2.3 copy-start.32
  164.9 151.5 %all-reduce.9.cloned.1.call-start = ((), (), s32[]{:S(2)}) async-start(), calls=%async_computation.8 | async-start | bytes 4194304 | tf_op jit(solution)/shard_map/psum | solution.py:613
  166.6 53.3 %copy-start.6 = (bf16[512,1024]{1,0:T(8,128)(2,1)}, bf16[512,1024]{1,0:T(8,128)(2,1)S(1)}, u32[]{:S(2)}) copy-start(bf16[512,1024]{1,0:T(8,128)(2,1)S(1)} %copy.58) | copy-start | bytes 3145732
  216.2 2.9 copy-start.1
  216.2 2.9 copy-start.13
  219.1 2.1 copy-start.17
  219.9 3.4 copy-start.8
  221.2 2.8 copy-start.11
  229.7 167.8 %reduce-scatter.8.cloned.1.call-start = ((), (), s32[]{:S(2)}) async-start(), calls=%async_computation.5 | async-start | bytes 7077888 | tf_op jit(solution)/shard_map/reduce_scatter | solution.py:701
  230.1 3.5 copy-start.10
  230.1 3.5 copy-start.33
  240.3 209.5 %reduce-scatter.12.cloned.1.call-start = ((), (), s32[]{:S(2)}) async-start(), calls=%async_computation.7 | async-start | bytes 7962624
  316.4 3.3 copy-start.14
  336.0 183.2 %reduce-scatter.10.cloned.1.call-start = ((), (), s32[]{:S(2)}) async-start(), calls=%async_computation.6 | async-start | bytes 7962624
  337.7 1.6 copy-start.3
  337.7 1.9 copy-start.7
  339.5 2.1 copy-start.15
  357.2 35.1 %slice-start = ((s8[6914048]{0:T(1024)(128)(4,1)}), s8[2719744]{0:T(1024)(128)(4,1)S(1)}, s32[]{:S(2)}) async-start(s8[6914048]{0:T(1024)(128)(4,1)} %bitcast.107), calls=%async_computation.9 | async-start | bytes 5439488
  383.3 9.0 %slice-start.1 = ((s8[6914048]{0:T(1024)(128)(4,1)}), s8[4194304]{0:T(1024)(128)(4,1)S(1)}, s32[]{:S(2)}) async-start(s8[6914048]{0:T(1024)(128)(4,1)} %bitcast.107), calls=%async_computation.10 | async-start | bytes 8388608
  383.3 9.0 %copy-start.22 = (bf16[512,1024]{1,0:T(8,128)(2,1)S(1)}, bf16[512,1024]{1,0:T(8,128)(2,1)}, u32[]{:S(2)}) copy-start(bf16[512,1024]{1,0:T(8,128)(2,1)} %copy-done.21) | copy-start | bytes 3145732
  (10 other events, 12.0 us)
Sparse Core Ops, SparseCore 0:
  103.7 50.8 all-reduce.4
  165.0 51.1 all-reduce.6
  229.9 86.4 all-reduce.8
  320.0 60.8 reduce-scatter.7
  384.3 65.5 reduce-scatter.11
  453.7 65.4 reduce-scatter.9
